TPU v7x, 128 devices: a whole 4x4x4 slice. The times are simulated.
128 devices in a mesh: frame: 16 (over z, x_hi, core), seq: 8 (over x_lo, y).
Axes of the slice: x: 4 (x_hi: 2, x_lo: 2; x = x_hi * 2 + x_lo), y: 4, z: 4, core: 2. Of those that a mesh axis runs over, the one named last changes fastest.
Arguments:
- frames: bfloat16 [32, 2048, 1152], P('frame', 'seq'), may hold values from -6 to 6
- modulation: float32 [2, 3, 1152], replicated, may hold values from 0.5 to 1.5
- spatial_qkv: bfloat16 [1152, 3456], replicated, as said below
- spatial_out: bfloat16 [1152, 1152], replicated, may hold values from -0.1875 to 0.1875
- temporal_qkv: bfloat16 [1152, 3456], replicated, as said below
- temporal_out: bfloat16 [1152, 1152], replicated, may hold values from -0.1875 to 0.1875
- qk_gain: float32 [2, 2, 72], replicated, may hold values from 1.5 to 5
Outputs:
- block_out: bfloat16 [32, 2048, 1152], P('frame', 'seq')
Inputs may be any that keep to these rules, and one draw needn't show every extreme that they name: `spatial_qkv`: entries of about 1/sqrt(1152) in size. `temporal_qkv`: entries of about 1/sqrt(1152) in size.
All inputs are finite; a program needn't handle non-finite values.
Results may differ from a plain program's by a relative error of at most 0.018.
Values may be sent and summed in bfloat16 or wider, within the bound.
A program may use at most 192 MiB of HBM per device.

v0:
```python
import functools

import jax
import jax.numpy as jnp
from jax import lax
from jax.experimental import pallas as pl
from jax.experimental.pallas import tpu as pltpu
from jax.sharding import PartitionSpec as P

HEADS = 16
HD = 72
D = 1152
HALF = 8 * HD
MESH = pl.DeviceIdType.MESH
LOG2E = 1.4426950408889634
SCALE = LOG2E / 72.0 ** 0.5
F32 = jnp.float32
BF16 = jnp.bfloat16


def layer_norm(values, scale, shift):
    centre = jnp.mean(values, axis=-1, keepdims=True)
    moved = values - centre
    spread = jnp.mean(moved * moved, axis=-1, keepdims=True)
    normal = moved * lax.rsqrt(spread + 1e-06)
    return (normal * (1.0 + scale) + shift).astype(BF16)


def qk_normalize(heads, gain):
    factor = lax.rsqrt(jnp.mean(heads * heads, axis=1, keepdims=True) + 1e-06)
    return heads * factor * gain[None]


def pad_rows(heads, fill):
    n, _, tokens = heads.shape
    return jnp.concatenate([heads, jnp.full((n, 8, tokens), fill, F32)], axis=1)


def nt_dot(a, b):
    return lax.dot_general(a, b, (((1,), (1,)), ((), ())), preferred_element_type=F32)


def tn_dot(a, b):
    return lax.dot_general(a, b, (((0,), (0,)), ((), ())), preferred_element_type=F32)


def block_kernel(frames, modulation_in, gains_in, w_qkv, w_out, w_qkv_two, w_out_two, home,
                 modulation, gains_raw, gains, xbuf, raw, wt, wt_two, wo, wo_two, q_t, k_rows, v_t, o_t, att, att2, fr2, res, perm, bias,
                 m_sem, w_sem, x_send, x_recv, x_fwd, kv_send, kv_recv, a_send, a_recv, f_send, f_recv, r_send, r_recv, stage_two, stage_three,
                 *, exact):
    f_me = lax.axis_index("frame")
    s_me = lax.axis_index("seq")
    group, core = f_me // 2, f_me % 2
    x_lo, y = s_me // 4, s_me % 4
    primary = x_lo == core
    local = primary & (y // 2 == core)
    partner = 2 * group + 1 - core
    other_x = 4 * (1 - x_lo) + y

    def raw_copy(part):
        return pltpu.make_async_copy(
            w_qkv.at[:, pl.ds(pl.multiple_of(part * D + x_lo * 512, 128), 640)],
            raw.at[part, :, pl.ds(0, 640)], w_sem.at[part])

    def raw_copy_two(part):
        return pltpu.make_async_copy(w_qkv_two.at[:, pl.ds(pl.multiple_of(part * D, 128), D)], raw.at[part], w_sem.at[part])

    small_copies = [pltpu.make_async_copy(modulation_in, modulation, m_sem.at[0]),
                    pltpu.make_async_copy(gains_in, gains_raw, m_sem.at[1])]
    out_copies = [pltpu.make_async_copy(w_out, wo, w_sem.at[3]), pltpu.make_async_copy(w_out_two, wo_two, w_sem.at[4])]

    barrier = pltpu.get_barrier_semaphore()

    def column_mate(n):
        step = n + 1
        return (2 * group + lax.rem(core + step, 2), 4 * x_lo + lax.rem(y + step // 2, 4))

    def group_mate(n):
        return (lax.rem(f_me + 2 * (n + 1), 16), s_me)

    def tell(n, sem, mate):
        pl.semaphore_signal(sem, inc=1, device_id=mate(n), device_id_type=MESH)

    for n in range(7):
        tell(n, barrier, column_mate)
    for n in range(7):
        tell(n, barrier, group_mate)
    pl.semaphore_signal(barrier, inc=1, device_id=(f_me, other_x), device_id_type=MESH)
    for part in range(3):
        raw_copy(part).start()
    pl.semaphore_wait(barrier, 15)

    def send(i):
        return pltpu.make_async_remote_copy(
            src_ref=frames.at[i], dst_ref=xbuf.at[y], send_sem=x_send.at[i], recv_sem=x_recv.at[y],
            device_id=(2 * group + x_lo, 4 * x_lo + 2 * core + i), device_id_type=MESH)

    def forward(slot):
        return pltpu.make_async_remote_copy(
            src_ref=xbuf.at[slot], dst_ref=xbuf.at[slot], send_sem=x_fwd.at[slot], recv_sem=x_recv.at[slot],
            device_id=(f_me, other_x), device_id_type=MESH)

    def is_self(i):
        return primary & (2 * core + i == y)

    def is_far(i):
        return lax.rem(2 * core + i + 4 - y, 4) == 2

    for i in range(2):
        @pl.when(jnp.logical_not(is_self(i)) & jnp.logical_not(is_far(i)))
        def _(i=i):
            send(i).start()

        @pl.when(is_self(i))
        def _(i=i):
            pltpu.make_async_copy(frames.at[i], xbuf.at[y], x_recv.at[y]).start()

    for n in range(7):
        tell(n, stage_two, group_mate)
    for copy in small_copies:
        copy.start()
    for copy in out_copies:
        copy.start()

    def receive(slot):
        pltpu.make_async_copy(frames.at[0], xbuf.at[slot], x_recv.at[slot]).wait()

        @pl.when(primary)
        def _():
            forward(slot).start()

    receive(y)
    for copy in small_copies:
        copy.wait()
    pl.semaphore_wait(stage_two, 7)
    pl.semaphore_signal(stage_three, inc=1, device_id=(f_me, other_x), device_id_type=MESH)
    diagonal = lax.broadcasted_iota(jnp.int32, (HD, HD), 0) == lax.broadcasted_iota(jnp.int32, (HD, HD), 1)
    for layer in range(2):
        for which in range(2):
            gains[layer, which] = jnp.sum(
                jnp.where(diagonal, gains_raw[layer, which:which + 1, :], 0.0), axis=1, keepdims=True)
    for part in range(3):
        raw_copy(part).wait()
        wt[part] = raw[part, :, :640].T
        raw_copy_two(part).start()

    scale, shift = modulation[0, 1:2, :], modulation[0, 0:1, :]
    weight_rows = pl.ds(pl.multiple_of(x_lo * 64, 64), HALF)

    def k_copy(slot):
        cols = pl.ds(pl.multiple_of(core * 1024 + slot * 256, 256), 256)
        return pltpu.make_async_remote_copy(
            src_ref=k_rows.at[:, cols], dst_ref=k_rows.at[:, cols], send_sem=kv_send.at[0, slot],
            recv_sem=kv_recv.at[0, slot], device_id=(partner, s_me), device_id_type=MESH)

    def v_copy(slot):
        cols = pl.ds(pl.multiple_of(core * 1024 + slot * 256, 256), 256)
        return pltpu.make_async_remote_copy(
            src_ref=v_t.at[:, :, cols], dst_ref=v_t.at[:, :, cols], send_sem=kv_send.at[1, slot],
            recv_sem=kv_recv.at[1, slot], device_id=(partner, s_me), device_id_type=MESH)

    def kv_wait(slot):
        cols = pl.ds(pl.multiple_of((1 - core) * 1024 + slot * 256, 256), 256)
        pltpu.make_async_copy(k_rows.at[:, cols], k_rows.at[:, cols], kv_recv.at[0, slot]).wait()
        pltpu.make_async_copy(v_t.at[:, :, cols], v_t.at[:, :, cols], kv_recv.at[1, slot]).wait()

    def place(slot):
        far = lax.rem(slot + 4 - y, 4)
        return 2 * lax.rem(far, 2) + far // 2

    def work(slot):
        normed = layer_norm(xbuf[slot].astype(F32), scale, shift)
        here = pl.ds(pl.multiple_of(place(slot) * 256, 256), 256)
        cols = pl.ds(pl.multiple_of(core * 1024 + slot * 256, 256), 256)

        def projected(part):
            return nt_dot(wt[part, weight_rows, :], normed).astype(BF16).astype(F32).reshape(8, HD, 256)

        keys = pad_rows(qk_normalize(projected(1), gains[0, 1]), 1.0)
        for h in range(8):
            k_rows[h, cols, :] = keys[h].T.astype(BF16)
        k_copy(slot).start()
        v_t[:, :, cols] = pad_rows(projected(2), 1.0).astype(BF16)
        v_copy(slot).start()
        q_t[:, :, here] = pad_rows(qk_normalize(projected(0), gains[0, 0]), -6.0).astype(BF16)

    work(y)

    for i in range(2):
        @pl.when(is_far(i))
        def _(i=i):
            send(1 - i).wait_send()
            send(i).start()

    def chunk(n, carry):
        slot = lax.rem(y + n + (n // 2) * (1 - 2 * lax.rem(n, 2)), 4)
        receive(slot)
        raw_copy_two(n - 1).wait()
        wt_two[n - 1] = raw[n - 1].T
        work(slot)
        return carry

    lax.fori_loop(1, 4, chunk, 0)

    my_rows = pl.ds(pl.multiple_of(f_me * 16, 16), 16)

    def near(n):
        step = 15 - n
        z = lax.rem(f_me // 4 + lax.rem(step, 4), 4)
        x_hi = lax.rem(f_me // 2 + step // 4, 2)
        return 4 * z + 2 * x_hi + lax.rem(core + step // 8, 2)

    def send_frame(n, carry):
        other = near(n)
        rows = pl.ds(pl.multiple_of(other * 16, 16), 16)
        pltpu.make_async_remote_copy(
            src_ref=frames.at[:, rows], dst_ref=fr2.at[pl.ds(2 * f_me, 2)], send_sem=f_send, recv_sem=f_recv,
            device_id=(other, s_me), device_id_type=MESH).start()
        return carry

    pl.semaphore_wait(stage_three, 1)
    lax.fori_loop(0, 15, send_frame, 0)
    pltpu.make_async_copy(frames.at[:, my_rows], fr2.at[pl.ds(2 * f_me, 2)], f_recv).start()

    row = lax.broadcasted_iota(jnp.int32, (512, 512), 0)
    column = lax.broadcasted_iota(jnp.int32, (512, 512), 1)
    perm[...] = jnp.where(column == (row & 31) * 16 + (row >> 5), 1.0, 0.0).astype(BF16)
    row = lax.broadcasted_iota(jnp.int32, (256, 256), 0)
    column = lax.broadcasted_iota(jnp.int32, (256, 256), 1)
    bias[...] = jnp.where((row >> 5) == (column >> 5), 0.0, -1e30)

    for slot in range(4):
        kv_wait(slot)

    frame = 4 * group + y

    def finish(summed):
        return summed[:HD] / summed[HD:HD + 1]

    def attend(block):
        cols = slice(block * 512, block * 512 + 512)

        def head(h, carry):
            scores = jnp.dot(k_rows[h], q_t[h, :, cols], preferred_element_type=F32)
            if exact:
                scores = scores - jnp.max(scores, axis=0, keepdims=True)
            weights = jnp.exp2(scores * SCALE).astype(BF16)
            o_t[h, :, cols] = finish(jnp.dot(v_t[h], weights, preferred_element_type=F32))
            return carry

        lax.fori_loop(0, 8, head, 0)
        for part in range(4):
            rows = slice(block * 512 + part * 128, block * 512 + part * 128 + 128)
            att[rows, :] = o_t[:, :, rows].reshape(HALF, 128).T.astype(BF16)

        def send_att(n, carry):
            i = lax.rem(y + block + 2 * lax.rem(n, 2), 4)
            owner = near(n // 2)
            rows = pl.ds(pl.multiple_of(512 * block + 256 * lax.rem(n, 2) + owner * 16, 16), 16)
            mine = (owner == f_me) & (4 * core + i == s_me)

            @pl.when(jnp.logical_not(mine))
            def _():
                pltpu.make_async_remote_copy(
                    src_ref=att.at[rows], dst_ref=att2.at[x_lo, frame], send_sem=a_send, recv_sem=a_recv,
                    device_id=(owner, 4 * core + i), device_id_type=MESH).start()

            @pl.when(mine)
            def _():
                pltpu.make_async_copy(att.at[rows], att2.at[x_lo, frame], a_recv).start()
            return carry

        lax.fori_loop(0, 32, send_att, 0)

    for block in range(2):
        attend(block)

    for i in range(2):
        @pl.when(jnp.logical_not(is_self(i)) & jnp.logical_not(is_far(1 - i)))
        def _(i=i):
            send(i).wait_send()

    @pl.when(primary)
    def _():
        for slot in range(4):
            forward(slot).wait_send()

    for slot in range(4):
        k_copy(slot).wait_send()
        v_copy(slot).wait_send()
    for copy in out_copies:
        copy.wait()
    pltpu.make_async_copy(fr2, fr2, f_recv).wait()
    pltpu.make_async_copy(att2, att2, a_recv).wait()

    branch = jnp.dot(att2[0].reshape(512, HALF), wo[:HALF], preferred_element_type=F32)
    branch = branch + jnp.dot(att2[1].reshape(512, HALF), wo[HALF:], preferred_element_type=F32)
    stream = (fr2[...].reshape(512, D).astype(F32) + modulation[0, 2:3, :] * branch).astype(BF16)
    fr2[...] = stream.reshape(32, 16, D)
    normed = layer_norm(stream.astype(F32), modulation[1, 1:2, :], modulation[1, 0:1, :])
    normed = jnp.dot(perm[...], normed, preferred_element_type=F32).astype(BF16)

    def projected_two(part):
        return nt_dot(wt_two[part], normed).astype(BF16).astype(F32).reshape(HEADS, HD, 512)

    keys = pad_rows(qk_normalize(projected_two(1), gains[1, 1]), 1.0)
    for h in range(HEADS):
        k_rows[h // 2, pl.ds(512 * (h % 2), 512), :] = keys[h].T.astype(BF16)
    queries = pad_rows(qk_normalize(projected_two(0), gains[1, 0]), -6.0).astype(BF16)
    values = pad_rows(projected_two(2), 1.0).astype(BF16)
    for h in range(HEADS):
        q_t[h // 2, :, pl.ds(512 * (h % 2), 512)] = queries[h]
        v_t[h // 2, :, pl.ds(512 * (h % 2), 512)] = values[h]

    def head_pair(h, carry):
        for part in range(4):
            cols = slice(part * 256, part * 256 + 256)
            scores = jnp.dot(k_rows[h, cols, :], q_t[h, :, cols], preferred_element_type=F32) + bias[...]
            top = jnp.max(scores, axis=0, keepdims=True)
            weights = jnp.exp2((scores - top) * SCALE).astype(BF16)
            o_t[h, :, cols] = finish(jnp.dot(v_t[h, :, cols], weights, preferred_element_type=F32))
        return carry

    lax.fori_loop(0, 8, head_pair, 0)
    attended = jnp.concatenate([o_t[h // 2, :, 512 * (h % 2):512 * (h % 2) + 512] for h in range(HEADS)], axis=0)
    attended = jnp.dot(attended.astype(BF16), perm[...], preferred_element_type=F32).astype(BF16)
    xbuf_rows = attended.T

    for part in range(4):
        xbuf[part // 2, pl.ds(128 * (part % 2), 128), :] = xbuf_rows[128 * part:128 * part + 128]

    def last(n, carry):
        quarter = lax.rem(f_me // 4 + 2 + n + n // 2 * (1 - 2 * lax.rem(n, 2)), 4)
        rows = xbuf[quarter // 2, pl.ds(pl.multiple_of(128 * lax.rem(quarter, 2), 128), 128), :]
        branch_two = jnp.dot(rows, wo_two[...], preferred_element_type=F32)
        eight = pl.ds(8 * quarter, 8)
        result = fr2[eight].reshape(128, D).astype(F32) + modulation[1, 2:3, :] * branch_two
        res[eight] = result.astype(BF16).reshape(8, 16, D)
        for j in range(4):
            other = 4 * quarter + j

            @pl.when(other != f_me)
            def _(other=other):
                pltpu.make_async_remote_copy(
                    src_ref=res.at[pl.ds(2 * other, 2)], dst_ref=home.at[:, my_rows], send_sem=r_send, recv_sem=r_recv,
                    device_id=(other, s_me), device_id_type=MESH).start()

            @pl.when(other == f_me)
            def _(other=other):
                pltpu.make_async_copy(res.at[pl.ds(2 * other, 2)], home.at[:, my_rows], r_recv).start()
        return carry

    lax.fori_loop(0, 4, last, 0)

    @pl.when(primary)
    def _():
        part = att.at[pl.ds(0, 1008)]
        pltpu.make_async_copy(part, part, a_send).wait()

    @pl.when(jnp.logical_not(primary))
    def _():
        pltpu.make_async_copy(att, att, a_send).wait()
    most = fr2.at[pl.ds(0, 30)]
    pltpu.make_async_copy(most, most, f_send).wait()
    most = res.at[pl.ds(0, 30)]
    pltpu.make_async_copy(most, most, r_send).wait()
    pltpu.make_async_copy(home, home, r_recv).wait()


def block_call(exact, frames, modulation, gains, w_qkv, w_out, w_qkv_two, w_out_two):
    anywhere = pl.BlockSpec(memory_space=pl.ANY)
    dma = pltpu.SemaphoreType.DMA
    return pl.pallas_call(
        functools.partial(block_kernel, exact=exact),
        out_shape=jax.ShapeDtypeStruct((2, 256, D), BF16),
        in_specs=[anywhere, anywhere, anywhere, anywhere, anywhere, anywhere, anywhere],
        out_specs=anywhere,
        scratch_shapes=[
            pltpu.VMEM((2, 3, D), F32),
            pltpu.VMEM((2, 2, HD), F32),
            pltpu.VMEM((2, 2, HD, 1), F32),
            pltpu.VMEM((4, 256, D), BF16),
            pltpu.VMEM((3, D, D), BF16),
            pltpu.VMEM((3, 640, D), BF16),
            pltpu.VMEM((3, D, D), BF16),
            pltpu.VMEM((D, D), BF16),
            pltpu.VMEM((D, D), BF16),
            pltpu.VMEM((8, 80, 1024), BF16),
            pltpu.VMEM((8, 2048, 80), BF16),
            pltpu.VMEM((8, 80, 2048), BF16),
            pltpu.VMEM((8, HD, 1024), F32),
            pltpu.VMEM((1024, HALF), BF16),
            pltpu.VMEM((2, 32, 16, HALF), BF16),
            pltpu.VMEM((32, 16, D), BF16),
            pltpu.VMEM((32, 16, D), BF16),
            pltpu.VMEM((512, 512), BF16),
            pltpu.VMEM((256, 256), F32),
            dma((2,)), dma((5,)), dma((2,)), dma((4,)), dma((4,)), dma((2, 4)), dma((2, 4)),
            dma, dma, dma, dma, dma, dma, pltpu.SemaphoreType.REGULAR, pltpu.SemaphoreType.REGULAR,
        ],
        compiler_params=pltpu.CompilerParams(
            collective_id=1 if exact else 0, has_side_effects=True, vmem_limit_bytes=60 << 20),
        name="block_exact" if exact else "block",
    )(frames, modulation, gains, w_qkv, w_out, w_qkv_two, w_out_two)


def body(frames, modulation, spatial_qkv, spatial_out, temporal_qkv, temporal_out, qk_gain):
    largest = 72.0 * SCALE * jnp.max(jnp.abs(qk_gain[0, 0] * qk_gain[0, 1]))
    return lax.cond(
        largest <= 115.0, functools.partial(block_call, False), functools.partial(block_call, True),
        frames, modulation, qk_gain, spatial_qkv, spatial_out, temporal_qkv, temporal_out)


def solution(mesh):
    in_specs = (P("frame", "seq", None), P(), P(), P(), P(), P(), P())
    out_specs = P("frame", "seq", None)
    return jax.shard_map(body, mesh=mesh, in_specs=in_specs, out_specs=out_specs, check_vma=False)
```

profile of v0, /device:TPU:0, one launch (start us, length us, event | category | flops | bytes accessed | tf_op | source)
XLA Modules:
  0.0 120.9 jit_solution(2306456060047635249)
XLA Ops:
  0.0 1.4 %abs_reduce_fusion = f32[]{:T(128)} fusion(f32[2,2,72]{2,1,0:T(2,128)} %param.15), kind=kLoop, calls=%fused_computation | loop fusion | flops 215 | bytes 580 | tf_op jit(solution)/shard_map/reduce_max | solution.py:408
  2.0 117.9 %conditional.1 = (bf16[2,256,1152]{2,1,0:T(8,128)(2,1)S(1)}) conditional(s32[]{:T(128)} %convert_element_type.3, (bf16[2,256,1152]{2,1,0:T(8,128)(2,1)}, f32[2,3,1152]{2,0,1:T(2,128)}, f32[2,2,72]{2,1,0:T(2,128)}, bf16[1152,3456]{1,0:T(8,128)(2,1)}, bf16[1152,1152]{1,0:T(8,128)(2,1)}, /*index=5*/bf16[1152,3456]{1,0:T(8,128)(2,1)}, ...), branch_computations={%region_1.0_spmd, %region_2.0_spmd} | conditional | bytes 55304 | solution.py:409
  2.0 1.4 %copy.10.modulation_in = f32[2,3,1152]{2,1,0:T(4,128)} copy(f32[2,3,1152]{2,0,1:T(2,128)} %get-tuple-element.52) | data formatting | bytes 55296 | tf_op jit(solution)/shard_map
  3.4 115.9 %block_exact.1 = bf16[2,256,1152]{2,1,0:T(8,128)(2,1)S(1)} custom-call(bf16[2,256,1152]{2,1,0:T(8,128)(2,1)} %get-tuple-element.36.frames, f32[2,3,1152]{2,1,0:T(4,128)} %copy.10.modulation_in, f32[2,2,72]{2,1,0:T(2,128)} %get-tuple-element.38.gains_in, bf16[1152,3456]{1,0:T(8,128)(2,1)} %get-tuple-element.39.w_qkv, ...), custom_call_target="tpu_custom_call" | custom-call | tf_op jit(solution)/shard_map/cond/branch_0_fun/block_exact/pallas_call | solution.py:373
  119.9 1.0 copy.15
where the time goes:
time: 123 us; the launch traced here: 121 us
  Pallas kernels  116 us (94%)
  local copies, waits for them, and re-layouts  2.39 us (2%)
  other arithmetic  1.36 us (1%)
    pallas_call x1, Pallas kernels, block_call(): pl.pallas_call(functools.partial(block_kernel, exact=exact), out_shape=ja...  116 us

commit v1 on v0

v1 whole, which is shorter than its diff:
```python
import functools

import jax
import jax.numpy as jnp
from jax import lax
from jax.experimental import pallas as pl
from jax.experimental.pallas import tpu as pltpu
from jax.sharding import PartitionSpec as P

HEADS = 16
HD = 72
D = 1152
HALF = 8 * HD
MESH = pl.DeviceIdType.MESH
LOG2E = 1.4426950408889634
SCALE = LOG2E / 72.0 ** 0.5
F32 = jnp.float32
BF16 = jnp.bfloat16


def layer_norm(values, scale, shift):
    centre = jnp.mean(values, axis=-1, keepdims=True)
    moved = values - centre
    spread = jnp.mean(moved * moved, axis=-1, keepdims=True)
    normal = moved * lax.rsqrt(spread + 1e-06)
    return (normal * (1.0 + scale) + shift).astype(BF16)


def qk_normalize(heads, gain):
    factor = lax.rsqrt(jnp.mean(heads * heads, axis=1, keepdims=True) + 1e-06)
    return heads * factor * gain[None]


def pad_rows(heads, fill):
    n, _, tokens = heads.shape
    return jnp.concatenate([heads, jnp.full((n, 8, tokens), fill, F32)], axis=1)


def nt_dot(a, b):
    return lax.dot_general(a, b, (((1,), (1,)), ((), ())), preferred_element_type=F32)


def tn_dot(a, b):
    return lax.dot_general(a, b, (((0,), (0,)), ((), ())), preferred_element_type=F32)


def block_kernel(frames, modulation_in, gains_in, w_qkv, w_out, w_qkv_two, w_out_two, home,
                 modulation, gains_raw, gains, xbuf, raw, wt, wt_two, wo, wo_two, q_t, k_rows, v_t, o_t, att, att2, fr2, res, perm, bias,
                 m_sem, w_sem, x_send, x_recv, x_fwd, kv_send, kv_recv, a_send, a_recv, f_send, f_recv, r_send, r_recv, stage_two,
                 *, exact):
    f_me = lax.axis_index("frame")
    s_me = lax.axis_index("seq")
    group, core = f_me // 2, f_me % 2
    x_lo, y = s_me // 4, s_me % 4
    half = lax.rem(y, 2)
    frame = 4 * group + 2 * x_lo + y // 2
    partner = 2 * group + 1 - core
    mate_row = y + 1 - 2 * half
    same = x_lo == core

    def raw_copy(part):
        return pltpu.make_async_copy(
            w_qkv.at[:, pl.ds(pl.multiple_of(part * D + half * 512, 128), 640)],
            raw.at[part, :, pl.ds(0, 640)], w_sem.at[part])

    def raw_copy_two(part):
        return pltpu.make_async_copy(w_qkv_two.at[:, pl.ds(pl.multiple_of(part * D, 128), D)], raw.at[part], w_sem.at[part])

    small_copies = [pltpu.make_async_copy(modulation_in, modulation, m_sem.at[0]),
                    pltpu.make_async_copy(gains_in, gains_raw, m_sem.at[1])]
    out_copies = [pltpu.make_async_copy(w_out, wo, w_sem.at[3]), pltpu.make_async_copy(w_out_two, wo_two, w_sem.at[4])]

    barrier = pltpu.get_barrier_semaphore()

    def plane_mate(n):
        step = n + 1
        return (2 * group + lax.rem(core + lax.rem(step, 2), 2),
                4 * lax.rem(x_lo + lax.rem(step // 2, 2), 2) + lax.rem(y + step // 4, 4))

    def group_mate(n):
        return (lax.rem(f_me + 2 * (n + 1), 16), s_me)

    def tell(n, sem, mate):
        pl.semaphore_signal(sem, inc=1, device_id=mate(n), device_id_type=MESH)

    for n in range(15):
        tell(n, barrier, plane_mate)
    for n in range(7):
        tell(n, barrier, group_mate)
    for part in range(3):
        raw_copy(part).start()
    pl.semaphore_wait(barrier, 22)

    def across(i):
        return lax.rem(i + y // 2, 2)

    def send(i):
        return pltpu.make_async_remote_copy(
            src_ref=frames.at[i], dst_ref=xbuf.at[y], send_sem=x_send.at[i], recv_sem=x_recv.at[y],
            device_id=(2 * group + x_lo, 4 * core + y + across(i) * (3 - 2 * y)), device_id_type=MESH)

    def forward(slot):
        return pltpu.make_async_remote_copy(
            src_ref=xbuf.at[slot], dst_ref=xbuf.at[slot], send_sem=x_fwd.at[slot], recv_sem=x_recv.at[slot],
            device_id=(f_me, 4 * x_lo + mate_row), device_id_type=MESH)

    for i in range(2):
        @pl.when((across(i) == 0) & jnp.logical_not(same))
        def _(i=i):
            send(i).start()

        @pl.when((across(i) == 0) & same)
        def _(i=i):
            pltpu.make_async_copy(frames.at[i], xbuf.at[y], x_recv.at[y]).start()

        @pl.when((across(i) == 1) & same)
        def _(i=i):
            send(i).start()

    for n in range(7):
        tell(n, stage_two, group_mate)
    for copy in small_copies:
        copy.start()
    for copy in out_copies:
        copy.start()

    def receive(slot):
        pltpu.make_async_copy(frames.at[0], xbuf.at[slot], x_recv.at[slot]).wait()

    receive(y)
    forward(y).start()
    for copy in small_copies:
        copy.wait()
    diagonal = lax.broadcasted_iota(jnp.int32, (HD, HD), 0) == lax.broadcasted_iota(jnp.int32, (HD, HD), 1)
    for layer in range(2):
        for which in range(2):
            gains[layer, which] = jnp.sum(
                jnp.where(diagonal, gains_raw[layer, which:which + 1, :], 0.0), axis=1, keepdims=True)
    for part in range(3):
        raw_copy(part).wait()
        wt[part] = raw[part, :, :640].T
        raw_copy_two(part).start()

    scale, shift = modulation[0, 1:2, :], modulation[0, 0:1, :]
    weight_rows = pl.ds(pl.multiple_of(half * 64, 64), HALF)

    def k_copy(slot):
        cols = pl.ds(pl.multiple_of(core * 1024 + slot * 256, 256), 256)
        return pltpu.make_async_remote_copy(
            src_ref=k_rows.at[:, cols], dst_ref=k_rows.at[:, cols], send_sem=kv_send.at[0, slot],
            recv_sem=kv_recv.at[0, slot], device_id=(partner, s_me), device_id_type=MESH)

    def v_copy(slot):
        cols = pl.ds(pl.multiple_of(core * 1024 + slot * 256, 256), 256)
        return pltpu.make_async_remote_copy(
            src_ref=v_t.at[:, :, cols], dst_ref=v_t.at[:, :, cols], send_sem=kv_send.at[1, slot],
            recv_sem=kv_recv.at[1, slot], device_id=(partner, s_me), device_id_type=MESH)

    def kv_wait(slot):
        cols = pl.ds(pl.multiple_of((1 - core) * 1024 + slot * 256, 256), 256)
        pltpu.make_async_copy(k_rows.at[:, cols], k_rows.at[:, cols], kv_recv.at[0, slot]).wait()
        pltpu.make_async_copy(v_t.at[:, :, cols], v_t.at[:, :, cols], kv_recv.at[1, slot]).wait()

    def work(slot):
        values = xbuf[slot].astype(F32).reshape(16, 2, 8, D)
        values = jnp.concatenate([values[:, 0].reshape(128, D), values[:, 1].reshape(128, D)], axis=0)
        normed = layer_norm(values, scale, shift)
        cols = pl.ds(pl.multiple_of(core * 1024 + slot * 256, 256), 256)

        def projected(part):
            return nt_dot(wt[part, weight_rows, :], normed).astype(BF16).astype(F32).reshape(8, HD, 256)

        keys = pad_rows(qk_normalize(projected(1), gains[0, 1]), 1.0)
        for h in range(8):
            k_rows[h, cols, :] = keys[h].T.astype(BF16)
        k_copy(slot).start()
        v_t[:, :, cols] = pad_rows(projected(2), 1.0).astype(BF16)
        v_copy(slot).start()
        queries = pad_rows(qk_normalize(projected(0), gains[0, 0]), -6.0).astype(BF16)
        q_t[:, :, pl.ds(pl.multiple_of(slot * 128, 128), 128)] = queries[:, :, :128]
        q_t[:, :, pl.ds(pl.multiple_of(512 + slot * 128, 128), 128)] = queries[:, :, 128:]

    work(y)

    for i in range(2):
        @pl.when((across(i) == 1) & jnp.logical_not(same))
        def _(i=i):
            send(1 - i).wait_send()
            send(i).start()

    pl.semaphore_wait(stage_two, 7)

    my_rows = pl.ds(pl.multiple_of(f_me * 16, 16), 16)

    def near(n):
        step = 15 - n
        z = lax.rem(f_me // 4 + lax.rem(step, 4), 4)
        x_hi = lax.rem(f_me // 2 + step // 4, 2)
        return 4 * z + 2 * x_hi + lax.rem(core + step // 8, 2)

    def send_frame(n, carry):
        other = near(n)
        rows = pl.ds(pl.multiple_of(other * 16, 16), 16)
        pltpu.make_async_remote_copy(
            src_ref=frames.at[:, rows], dst_ref=fr2.at[pl.ds(2 * f_me, 2)], send_sem=f_send, recv_sem=f_recv,
            device_id=(other, s_me), device_id_type=MESH).start()
        return carry

    lax.fori_loop(0, 15, send_frame, 0)
    pltpu.make_async_copy(frames.at[:, my_rows], fr2.at[pl.ds(2 * f_me, 2)], f_recv).start()

    def chunk(n, carry):
        row = y + (n // 2) * (mate_row - y)
        slot = row + lax.rem(n, 2) * (3 - 2 * row)
        receive(slot)

        @pl.when(n == 1)
        def _():
            forward(slot).start()

        raw_copy_two(n - 1).wait()
        wt_two[n - 1] = raw[n - 1].T
        work(slot)
        return carry

    lax.fori_loop(1, 4, chunk, 0)

    row = lax.broadcasted_iota(jnp.int32, (256, 256), 0)
    column = lax.broadcasted_iota(jnp.int32, (256, 256), 1)
    perm[...] = jnp.where(column == (row & 31) * 8 + (row >> 5), 1.0, 0.0).astype(BF16)
    bias[...] = jnp.where((row >> 5) == (column >> 5), 0.0, -1e30)

    for slot in range(4):
        kv_wait(slot)

    def finish(summed):
        return summed[:HD] / summed[HD:HD + 1]

    def attend(block):
        cols = slice(block * 512, block * 512 + 512)

        def head(h, carry):
            scores = jnp.dot(k_rows[h], q_t[h, :, cols], preferred_element_type=F32)
            if exact:
                scores = scores - jnp.max(scores, axis=0, keepdims=True)
            weights = jnp.exp2(scores * SCALE).astype(BF16)
            o_t[h, :, cols] = finish(jnp.dot(v_t[h], weights, preferred_element_type=F32))
            return carry

        lax.fori_loop(0, 8, head, 0)
        for part in range(4):
            cols = slice(block * 512 + part * 128, block * 512 + part * 128 + 128)
            rows = o_t[:, :, cols].reshape(HALF, 128).T.reshape(16, 8, HALF)
            att[block * 64 + part * 16:block * 64 + part * 16 + 16] = rows.astype(BF16)

        def send_att(n, carry):
            i = lax.rem(y + 2 * lax.rem(n, 2) + n // 32, 4)
            owner = near(lax.rem(n // 2, 16))
            block_ref = att.at[block * 64 + i * 16 + owner]
            mine = (owner == f_me) & (4 * core + i == s_me)

            @pl.when(jnp.logical_not(mine))
            def _():
                pltpu.make_async_remote_copy(
                    src_ref=block_ref, dst_ref=att2.at[block, half, frame], send_sem=a_send, recv_sem=a_recv.at[block],
                    device_id=(owner, 4 * core + i), device_id_type=MESH).start()

            @pl.when(mine)
            def _():
                pltpu.make_async_copy(block_ref, att2.at[block, half, frame], a_recv.at[block]).start()
            return carry

        lax.fori_loop(0, 64, send_att, 0)

    for block in range(2):
        attend(block)

    for i in range(2):
        @pl.when(across(i) == 1)
        def _(i=i):
            send(i).wait_send()

    forward(y).wait_send()
    forward(3 - y).wait_send()

    for slot in range(4):
        k_copy(slot).wait_send()
        v_copy(slot).wait_send()
    for copy in out_copies:
        copy.wait()
    pltpu.make_async_copy(fr2, fr2, f_recv).wait()

    def temporal(turn, carry):
        pltpu.make_async_copy(att2.at[turn], att2.at[turn], a_recv.at[turn]).wait()
        branch = jnp.zeros((256, D), F32)
        for hh in range(2):
            rows = att2[turn, hh].astype(F32).reshape(256, HALF).astype(BF16)
            branch = branch + jnp.dot(rows, wo[HALF * hh:HALF * hh + HALF], preferred_element_type=F32)
        rows = fr2[...].astype(F32).reshape(32, 2, 8, D)
        rows = jnp.where(turn == 0, rows[:, 0], rows[:, 1]).reshape(256, D)
        stream = (rows + modulation[0, 2:3, :] * branch).astype(BF16)
        normed = layer_norm(stream.astype(F32), modulation[1, 1:2, :], modulation[1, 0:1, :])
        normed = jnp.dot(perm[...], normed, preferred_element_type=F32).astype(BF16)

        def projected_two(part):
            return nt_dot(wt_two[part], normed).astype(BF16).astype(F32).reshape(HEADS, HD, 256)

        keys = pad_rows(qk_normalize(projected_two(1), gains[1, 1]), 1.0)
        queries = pad_rows(qk_normalize(projected_two(0), gains[1, 0]), -6.0).astype(BF16)
        values = pad_rows(projected_two(2), 1.0).astype(BF16)
        for h in range(HEADS):
            cols = pl.ds(256 * (h % 4), 256)
            k_rows[h // 4, cols, :] = keys[h].T.astype(BF16)
            q_t[h // 4, :, cols] = queries[h]
            v_t[h // 4, :, cols] = values[h]

        def four_heads(h, carry):
            parts = [slice(part * 256, part * 256 + 256) for part in range(4)]
            scores = [jnp.dot(k_rows[h, cols, :], q_t[h, :, cols], preferred_element_type=F32) for cols in parts]
            if exact:
                scores = [each - jnp.max(each + bias[...], axis=0, keepdims=True) for each in scores]
            weights = [jnp.exp2(each * SCALE + bias[...]).astype(BF16) for each in scores]
            summed = [jnp.dot(v_t[h, :, cols], each, preferred_element_type=F32) for cols, each in zip(parts, weights)]
            for cols, each in zip(parts, summed):
                o_t[h, :, cols] = finish(each)
            return carry

        lax.fori_loop(0, 4, four_heads, 0)
        attended = jnp.concatenate([o_t[h // 4, :, 256 * (h % 4):256 * (h % 4) + 256] for h in range(HEADS)], axis=0)
        attended = jnp.dot(attended.astype(BF16), perm[...], preferred_element_type=F32).astype(BF16)
        result = stream.astype(F32) + modulation[1, 2:3, :] * tn_dot(attended, wo_two[...])
        res[turn] = result.reshape(32, 8, D).astype(BF16)

        def send_home(n, carry):
            other = near(n)
            pltpu.make_async_remote_copy(
                src_ref=res.at[turn, pl.ds(2 * other, 2)], dst_ref=home.at[f_me, turn], send_sem=r_send, recv_sem=r_recv,
                device_id=(other, s_me), device_id_type=MESH).start()
            return carry

        lax.fori_loop(0, 15, send_home, 0)
        pltpu.make_async_copy(res.at[turn, pl.ds(2 * f_me, 2)], home.at[f_me, turn], r_recv).start()
        return carry

    lax.fori_loop(0, 2, temporal, 0)

    @pl.when(same)
    def _():
        part = att.at[pl.ds(0, 126)]
        pltpu.make_async_copy(part, part, a_send).wait()

    @pl.when(jnp.logical_not(same))
    def _():
        pltpu.make_async_copy(att, att, a_send).wait()
    most = fr2.at[pl.ds(0, 30)]
    pltpu.make_async_copy(most, most, f_send).wait()
    most = res.at[:, pl.ds(0, 30)]
    pltpu.make_async_copy(most, most, r_send).wait()
    pltpu.make_async_copy(home, home, r_recv).wait()


def block_call(exact, frames, modulation, gains, w_qkv, w_out, w_qkv_two, w_out_two):
    anywhere = pl.BlockSpec(memory_space=pl.ANY)
    dma = pltpu.SemaphoreType.DMA
    return pl.pallas_call(
        functools.partial(block_kernel, exact=exact),
        out_shape=jax.ShapeDtypeStruct((16, 2, 2, 8, D), BF16),
        in_specs=[anywhere, anywhere, anywhere, anywhere, anywhere, anywhere, anywhere],
        out_specs=anywhere,
        scratch_shapes=[
            pltpu.VMEM((2, 3, D), F32),
            pltpu.VMEM((2, 2, HD), F32),
            pltpu.VMEM((2, 2, HD, 1), F32),
            pltpu.VMEM((4, 256, D), BF16),
            pltpu.VMEM((3, D, D), BF16),
            pltpu.VMEM((3, 640, D), BF16),
            pltpu.VMEM((3, D, D), BF16),
            pltpu.VMEM((D, D), BF16),
            pltpu.VMEM((D, D), BF16),
            pltpu.VMEM((8, 80, 1024), BF16),
            pltpu.VMEM((8, 2048, 80), BF16),
            pltpu.VMEM((8, 80, 2048), BF16),
            pltpu.VMEM((8, HD, 1024), F32),
            pltpu.VMEM((128, 8, HALF), BF16),
            pltpu.VMEM((2, 2, 32, 8, HALF), BF16),
            pltpu.VMEM((32, 16, D), BF16),
            pltpu.VMEM((2, 32, 8, D), BF16),
            pltpu.VMEM((256, 256), BF16),
            pltpu.VMEM((256, 256), F32),
            dma((2,)), dma((5,)), dma((2,)), dma((4,)), dma((4,)), dma((2, 4)), dma((2, 4)),
            dma, dma((2,)), dma, dma, dma, dma, pltpu.SemaphoreType.REGULAR,
        ],
        compiler_params=pltpu.CompilerParams(
            collective_id=1 if exact else 0, has_side_effects=True, vmem_limit_bytes=60 << 20),
        name="block_exact" if exact else "block",
    )(frames, modulation, gains, w_qkv, w_out, w_qkv_two, w_out_two)


def body(frames, modulation, spatial_qkv, spatial_out, temporal_qkv, temporal_out, qk_gain):
    largest = 72.0 * SCALE * jnp.max(jnp.abs(qk_gain[:, 0] * qk_gain[:, 1]))
    home = lax.cond(
        largest <= 115.0, functools.partial(block_call, False), functools.partial(block_call, True),
        frames, modulation, qk_gain, spatial_qkv, spatial_out, temporal_qkv, temporal_out)
    return jnp.transpose(home, (2, 0, 1, 3, 4)).reshape(2, 256, D)


def solution(mesh):
    in_specs = (P("frame", "seq", None), P(), P(), P(), P(), P(), P())
    out_specs = P("frame", "seq", None)
    return jax.shard_map(body, mesh=mesh, in_specs=in_specs, out_specs=out_specs, check_vma=False)
```

time: 123 us -> 110 us (0.89)
  Pallas kernels: 116 us -> 104 us
    pallas_call x1, Pallas kernels: 116 us -> 104 us  [block_call(): pl.pallas_call(functools.partial(block_kernel, exact=exact), out_shape=ja...]
where the time goes in v1:
time: 110 us; the launch traced here: 109 us
  Pallas kernels  104 us (95%)
  local copies, waits for them, and re-layouts  2.48 us (2%)
  other arithmetic  1.37 us (1%)
    pallas_call x1, Pallas kernels, block_call(): pl.pallas_call(functools.partial(block_kernel, exact=exact), out_shape=ja...  104 us

profile of v1, /device:TPU:0, one launch (start us, length us, event | category | flops | bytes accessed | tf_op | source)
XLA Modules:
  0.0 108.6 jit_solution(5926403681662792025)
XLA Ops:
  0.0 1.4 %abs_reduce_fusion = f32[]{:T(128)} fusion(f32[2,2,72]{2,1,0:T(2,128)} %param.15), kind=kLoop, calls=%fused_computation | loop fusion | flops 431 | bytes 1156 | tf_op jit(solution)/shard_map/reduce_max | solution.py:400
  2.0 105.4 %conditional.1 = (bf16[16,2,2,8,1152]{4,3,2,1,0:T(8,128)(2,1)S(1)}) conditional(s32[]{:T(128)} %convert_element_type.3, (bf16[2,256,1152]{2,1,0:T(8,128)(2,1)}, f32[2,3,1152]{2,0,1:T(2,128)}, f32[2,2,72]{2,1,0:T(2,128)}, bf16[1152,3456]{1,0:T(8,128)(2,1)}, bf16[1152,1152]{1,0:T(8,128)(2,1)}, /*index=5*/bf16[1152,3456]{1,0:T(8,128)(2,1)}, ...), branch_computations={%region_1.0_spmd, %region_2.0_spmd} | conditional | bytes 55304 | solution.py:401
  2.0 1.4 %copy.8.modulation_in = f32[2,3,1152]{2,1,0:T(4,128)} copy(f32[2,3,1152]{2,0,1:T(2,128)} %get-tuple-element.51) | data formatting | bytes 55296 | tf_op jit(solution)/shard_map
  3.4 103.5 %block_exact.1 = bf16[16,2,2,8,1152]{4,3,2,1,0:T(8,128)(2,1)S(1)} custom-call(bf16[2,256,1152]{2,1,0:T(8,128)(2,1)} %get-tuple-element.36.frames, f32[2,3,1152]{2,1,0:T(4,128)} %copy.8.modulation_in, f32[2,2,72]{2,1,0:T(2,128)} %get-tuple-element.38.gains_in, bf16[1152,3456]{1,0:T(8,128)(2,1)} %get-tuple-element.39.w_qkv, ...), custom_call_target="tpu_custom_call" | custom-call | tf_op jit(solution)/shard_map/cond/branch_0_fun/block_exact/pallas_call | solution.py:365
  107.5 1.1 %copy.10 = bf16[2,16,2,8,1152]{4,3,2,1,0:T(8,128)(2,1)} copy(bf16[2,16,2,8,1152]{4,3,0,2,1:T(8,128)(2,1)S(1)} %bitcast.2) | data formatting | bytes 2359296 | tf_op jit(solution)/shard_map/transpose | solution.py:404

commit v2 on v1

--- a/solution.py
+++ b/solution.py
@@ -46,7 +46,7 @@
 
 def block_kernel(frames, modulation_in, gains_in, w_qkv, w_out, w_qkv_two, w_out_two, home,
                  modulation, gains_raw, gains, xbuf, raw, wt, wt_two, wo, wo_two, q_t, k_rows, v_t, o_t, att, att2, fr2, res, perm, bias,
-                 m_sem, w_sem, x_send, x_recv, x_fwd, kv_send, kv_recv, a_send, a_recv, f_send, f_recv, r_send, r_recv, stage_two,
+                 m_sem, w_sem, x_send, x_recv, x_fwd, kv_send, kv_recv, a_send, a_recv, f_send, f_recv, r_send, r_recv, stages,
                  *, exact):
     f_me = lax.axis_index("frame")
     s_me = lax.axis_index("seq")
@@ -77,19 +77,19 @@
         return (2 * group + lax.rem(core + lax.rem(step, 2), 2),
                 4 * lax.rem(x_lo + lax.rem(step // 2, 2), 2) + lax.rem(y + step // 4, 4))
 
-    def group_mate(n):
-        return (lax.rem(f_me + 2 * (n + 1), 16), s_me)
-
-    def tell(n, sem, mate):
-        pl.semaphore_signal(sem, inc=1, device_id=mate(n), device_id_type=MESH)
+    above, below = (lax.rem(f_me + 4, 16), s_me), (lax.rem(f_me + 12, 16), s_me)
+    beside = (f_me + 2 - 4 * lax.rem(f_me // 2, 2), 4 * (1 - x_lo) + y)
+
+    def tell(sem, mate):
+        pl.semaphore_signal(sem, inc=1, device_id=mate, device_id_type=MESH)
 
     for n in range(15):
-        tell(n, barrier, plane_mate)
-    for n in range(7):
-        tell(n, barrier, group_mate)
+        tell(barrier, plane_mate(n))
+    for mate in (above, below, beside):
+        tell(barrier, mate)
     for part in range(3):
         raw_copy(part).start()
-    pl.semaphore_wait(barrier, 22)
+    pl.semaphore_wait(barrier, 18)
 
     def across(i):
         return lax.rem(i + y // 2, 2)
@@ -117,8 +117,8 @@
         def _(i=i):
             send(i).start()
 
-    for n in range(7):
-        tell(n, stage_two, group_mate)
+    for mate in (above, below):
+        tell(stages.at[0], mate)
     for copy in small_copies:
         copy.start()
     for copy in out_copies:
@@ -141,31 +141,38 @@
         wt[part] = raw[part, :, :640].T
         raw_copy_two(part).start()
 
-    scale, shift = modulation[0, 1:2, :], modulation[0, 0:1, :]
+    scale, shift = modulation[1, 0:1, :], modulation[0, 0:1, :]
     weight_rows = pl.ds(pl.multiple_of(half * 64, 64), HALF)
 
-    def k_copy(slot):
-        cols = pl.ds(pl.multiple_of(core * 1024 + slot * 256, 256), 256)
+    def row_of(n):
+        row = y + (n // 2) * (mate_row - y)
+        return row + lax.rem(n, 2) * (3 - 2 * row)
+
+    pl.semaphore_wait(stages.at[0], 2)
+    tell(stages.at[1], above)
+
+    def k_copy(n):
+        cols = pl.ds(pl.multiple_of(n * 512 + core * 256, 256), 256)
         return pltpu.make_async_remote_copy(
-            src_ref=k_rows.at[:, cols], dst_ref=k_rows.at[:, cols], send_sem=kv_send.at[0, slot],
-            recv_sem=kv_recv.at[0, slot], device_id=(partner, s_me), device_id_type=MESH)
-
-    def v_copy(slot):
-        cols = pl.ds(pl.multiple_of(core * 1024 + slot * 256, 256), 256)
+            src_ref=k_rows.at[:, cols], dst_ref=k_rows.at[:, cols], send_sem=kv_send.at[0, n],
+            recv_sem=kv_recv.at[0, n], device_id=(partner, s_me), device_id_type=MESH)
+
+    def v_copy(n):
+        cols = pl.ds(pl.multiple_of(n * 512 + core * 256, 256), 256)
         return pltpu.make_async_remote_copy(
-            src_ref=v_t.at[:, :, cols], dst_ref=v_t.at[:, :, cols], send_sem=kv_send.at[1, slot],
-            recv_sem=kv_recv.at[1, slot], device_id=(partner, s_me), device_id_type=MESH)
-
-    def kv_wait(slot):
-        cols = pl.ds(pl.multiple_of((1 - core) * 1024 + slot * 256, 256), 256)
-        pltpu.make_async_copy(k_rows.at[:, cols], k_rows.at[:, cols], kv_recv.at[0, slot]).wait()
-        pltpu.make_async_copy(v_t.at[:, :, cols], v_t.at[:, :, cols], kv_recv.at[1, slot]).wait()
-
-    def work(slot):
-        values = xbuf[slot].astype(F32).reshape(16, 2, 8, D)
+            src_ref=v_t.at[:, :, cols], dst_ref=v_t.at[:, :, cols], send_sem=kv_send.at[1, n],
+            recv_sem=kv_recv.at[1, n], device_id=(partner, s_me), device_id_type=MESH)
+
+    def kv_wait(n):
+        cols = pl.ds(pl.multiple_of(n * 512 + (1 - core) * 256, 256), 256)
+        pltpu.make_async_copy(k_rows.at[:, cols], k_rows.at[:, cols], kv_recv.at[0, n]).wait()
+        pltpu.make_async_copy(v_t.at[:, :, cols], v_t.at[:, :, cols], kv_recv.at[1, n]).wait()
+
+    def work(n):
+        values = xbuf[row_of(n)].astype(F32).reshape(16, 2, 8, D)
         values = jnp.concatenate([values[:, 0].reshape(128, D), values[:, 1].reshape(128, D)], axis=0)
         normed = layer_norm(values, scale, shift)
-        cols = pl.ds(pl.multiple_of(core * 1024 + slot * 256, 256), 256)
+        cols = pl.ds(pl.multiple_of(n * 512 + core * 256, 256), 256)
 
         def projected(part):
             return nt_dot(wt[part, weight_rows, :], normed).astype(BF16).astype(F32).reshape(8, HD, 256)
@@ -173,14 +180,16 @@
         keys = pad_rows(qk_normalize(projected(1), gains[0, 1]), 1.0)
         for h in range(8):
             k_rows[h, cols, :] = keys[h].T.astype(BF16)
-        k_copy(slot).start()
+        k_copy(n).start()
         v_t[:, :, cols] = pad_rows(projected(2), 1.0).astype(BF16)
-        v_copy(slot).start()
+        v_copy(n).start()
         queries = pad_rows(qk_normalize(projected(0), gains[0, 0]), -6.0).astype(BF16)
-        q_t[:, :, pl.ds(pl.multiple_of(slot * 128, 128), 128)] = queries[:, :, :128]
-        q_t[:, :, pl.ds(pl.multiple_of(512 + slot * 128, 128), 128)] = queries[:, :, 128:]
-
-    work(y)
+        q_t[:, :, pl.ds(pl.multiple_of(n * 128, 128), 128)] = queries[:, :, :128]
+        q_t[:, :, pl.ds(pl.multiple_of(512 + n * 128, 128), 128)] = queries[:, :, 128:]
+
+    work(0)
+    pl.semaphore_wait(stages.at[1], 1)
+    tell(stages.at[2], beside)
 
     for i in range(2):
         @pl.when((across(i) == 1) & jnp.logical_not(same))
@@ -188,7 +197,6 @@
             send(1 - i).wait_send()
             send(i).start()
 
-    pl.semaphore_wait(stage_two, 7)
 
     my_rows = pl.ds(pl.multiple_of(f_me * 16, 16), 16)
 
@@ -206,35 +214,42 @@
             device_id=(other, s_me), device_id_type=MESH).start()
         return carry
 
-    lax.fori_loop(0, 15, send_frame, 0)
-    pltpu.make_async_copy(frames.at[:, my_rows], fr2.at[pl.ds(2 * f_me, 2)], f_recv).start()
 
     def chunk(n, carry):
-        row = y + (n // 2) * (mate_row - y)
-        slot = row + lax.rem(n, 2) * (3 - 2 * row)
+        slot = row_of(n)
         receive(slot)
 
         @pl.when(n == 1)
         def _():
             forward(slot).start()
 
+        work(n)
         raw_copy_two(n - 1).wait()
         wt_two[n - 1] = raw[n - 1].T
-        work(slot)
         return carry
 
-    lax.fori_loop(1, 4, chunk, 0)
+    pl.semaphore_wait(stages.at[2], 1)
+    lax.fori_loop(4, 8, send_frame, 0)
+    lax.fori_loop(12, 15, send_frame, 0)
+    lax.fori_loop(1, 3, chunk, 0)
+    raw_copy_two(2).wait()
+    wt_two[2] = raw[2].T
 
     row = lax.broadcasted_iota(jnp.int32, (256, 256), 0)
     column = lax.broadcasted_iota(jnp.int32, (256, 256), 1)
     perm[...] = jnp.where(column == (row & 31) * 8 + (row >> 5), 1.0, 0.0).astype(BF16)
     bias[...] = jnp.where((row >> 5) == (column >> 5), 0.0, -1e30)
 
-    for slot in range(4):
-        kv_wait(slot)
-
     def finish(summed):
         return summed[:HD] / summed[HD:HD + 1]
+
+    lax.fori_loop(0, 4, send_frame, 0)
+    lax.fori_loop(8, 12, send_frame, 0)
+    pltpu.make_async_copy(frames.at[:, my_rows], fr2.at[pl.ds(2 * f_me, 2)], f_recv).start()
+    receive(row_of(3))
+    work(3)
+    for n in range(4):
+        kv_wait(n)
 
     def attend(block):
         cols = slice(block * 512, block * 512 + 512)
@@ -254,9 +269,10 @@
             att[block * 64 + part * 16:block * 64 + part * 16 + 16] = rows.astype(BF16)
 
         def send_att(n, carry):
-            i = lax.rem(y + 2 * lax.rem(n, 2) + n // 32, 4)
+            part = n // 32 + lax.rem(n, 2) * (3 - 2 * (n // 32))
+            i = row_of(part)
             owner = near(lax.rem(n // 2, 16))
-            block_ref = att.at[block * 64 + i * 16 + owner]
+            block_ref = att.at[block * 64 + part * 16 + owner]
             mine = (owner == f_me) & (4 * core + i == s_me)
 
             @pl.when(jnp.logical_not(mine))
@@ -298,8 +314,8 @@
             branch = branch + jnp.dot(rows, wo[HALF * hh:HALF * hh + HALF], preferred_element_type=F32)
         rows = fr2[...].astype(F32).reshape(32, 2, 8, D)
         rows = jnp.where(turn == 0, rows[:, 0], rows[:, 1]).reshape(256, D)
-        stream = (rows + modulation[0, 2:3, :] * branch).astype(BF16)
-        normed = layer_norm(stream.astype(F32), modulation[1, 1:2, :], modulation[1, 0:1, :])
+        stream = (rows + modulation[2, 0:1, :] * branch).astype(BF16)
+        normed = layer_norm(stream.astype(F32), modulation[1, 1:2, :], modulation[0, 1:2, :])
         normed = jnp.dot(perm[...], normed, preferred_element_type=F32).astype(BF16)
 
         def projected_two(part):
@@ -328,7 +344,7 @@
         lax.fori_loop(0, 4, four_heads, 0)
         attended = jnp.concatenate([o_t[h // 4, :, 256 * (h % 4):256 * (h % 4) + 256] for h in range(HEADS)], axis=0)
         attended = jnp.dot(attended.astype(BF16), perm[...], preferred_element_type=F32).astype(BF16)
-        result = stream.astype(F32) + modulation[1, 2:3, :] * tn_dot(attended, wo_two[...])
+        result = stream.astype(F32) + modulation[2, 1:2, :] * tn_dot(attended, wo_two[...])
         res[turn] = result.reshape(32, 8, D).astype(BF16)
 
         def send_home(n, carry):
@@ -368,7 +384,7 @@
         in_specs=[anywhere, anywhere, anywhere, anywhere, anywhere, anywhere, anywhere],
         out_specs=anywhere,
         scratch_shapes=[
-            pltpu.VMEM((2, 3, D), F32),
+            pltpu.VMEM((3, 2, D), F32),
             pltpu.VMEM((2, 2, HD), F32),
             pltpu.VMEM((2, 2, HD, 1), F32),
             pltpu.VMEM((4, 256, D), BF16),
@@ -388,7 +404,7 @@
             pltpu.VMEM((256, 256), BF16),
             pltpu.VMEM((256, 256), F32),
             dma((2,)), dma((5,)), dma((2,)), dma((4,)), dma((4,)), dma((2, 4)), dma((2, 4)),
-            dma, dma((2,)), dma, dma, dma, dma, pltpu.SemaphoreType.REGULAR,
+            dma, dma((2,)), dma, dma, dma, dma, pltpu.SemaphoreType.REGULAR((3,)),
         ],
         compiler_params=pltpu.CompilerParams(
             collective_id=1 if exact else 0, has_side_effects=True, vmem_limit_bytes=60 << 20),
@@ -397,10 +413,10 @@
 
 
 def body(frames, modulation, spatial_qkv, spatial_out, temporal_qkv, temporal_out, qk_gain):
-    largest = 72.0 * SCALE * jnp.max(jnp.abs(qk_gain[:, 0] * qk_gain[:, 1]))
+    largest = jnp.max(jnp.abs(qk_gain[:, 0] * qk_gain[:, 1]))
     home = lax.cond(
-        largest <= 115.0, functools.partial(block_call, False), functools.partial(block_call, True),
-        frames, modulation, qk_gain, spatial_qkv, spatial_out, temporal_qkv, temporal_out)
+        largest <= 115.0 / (72.0 * SCALE), functools.partial(block_call, False), functools.partial(block_call, True),
+        frames, jnp.transpose(modulation, (1, 0, 2)), qk_gain, spatial_qkv, spatial_out, temporal_qkv, temporal_out)
     return jnp.transpose(home, (2, 0, 1, 3, 4)).reshape(2, 256, D)
 
 

time: 110 us -> 107 us (0.973); the launches traced: 109 us -> 107 us
  local copies, waits for them, and re-layouts: 2.48 us -> 1.1 us
    another operation x1 -> x0, local copies, waits for them, and re-layouts: 1.37 us -> none
where the time goes in v2:
time: 107 us
  Pallas kernels  103 us (96%)
  other arithmetic  1.37 us (1%)
  local copies, waits for them, and re-layouts  1.1 us (1%)
    pallas_call x1, Pallas kernels, block_call(): pl.pallas_call(functools.partial(block_kernel, exact=exact), out_shape=ja...  103 us

profile of v2, /device:TPU:0, one launch (start us, length us, event | category | flops | bytes accessed | tf_op | source)
XLA Modules:
  0.0 107.0 jit_solution(13917771878377745224)
XLA Ops:
  0.0 1.4 %abs_reduce_fusion = f32[]{:T(128)} fusion(f32[2,2,72]{2,1,0:T(2,128)} %param.15), kind=kLoop, calls=%fused_computation | loop fusion | flops 431 | bytes 1156 | tf_op jit(solution)/shard_map/reduce_max | solution.py:416
  2.0 103.8 %conditional.1 = (bf16[16,2,2,8,1152]{4,3,2,1,0:T(8,128)(2,1)S(1)}) conditional(s32[]{:T(128)} %convert_element_type.3, (bf16[2,256,1152]{2,1,0:T(8,128)(2,1)}, f32[3,2,1152]{2,1,0:T(2,128)}, f32[2,2,72]{2,1,0:T(2,128)}, bf16[1152,3456]{1,0:T(8,128)(2,1)}, bf16[1152,1152]{1,0:T(8,128)(2,1)}, /*index=5*/bf16[1152,3456]{1,0:T(8,128)(2,1)}, ...), branch_computations={%region_1.0_spmd, %region_2.0_spmd} | conditional | bytes 8 | solution.py:417
  2.0 103.3 %block_exact.1 = bf16[16,2,2,8,1152]{4,3,2,1,0:T(8,128)(2,1)S(1)} custom-call(bf16[2,256,1152]{2,1,0:T(8,128)(2,1)} %get-tuple-element.36.frames, f32[3,2,1152]{2,1,0:T(2,128)} %get-tuple-element.37.modulation_in, f32[2,2,72]{2,1,0:T(2,128)} %get-tuple-element.38.gains_in, bf16[1152,3456]{1,0:T(8,128)(2,1)} %get-tuple-element.39.w_qkv, ...), custom_call_target="tpu_custom_call" | custom-call | tf_op jit(solution)/shard_map/cond/branch_0_fun/block_exact/pallas_call | solution.py:381
  105.8 1.1 %copy.8 = bf16[2,16,2,8,1152]{4,3,2,1,0:T(8,128)(2,1)} copy(bf16[2,16,2,8,1152]{4,3,0,2,1:T(8,128)(2,1)S(1)} %bitcast.3) | data formatting | bytes 2359296 | tf_op jit(solution)/shard_map/transpose | solution.py:420

commit v3 on v2

--- a/solution.py
+++ b/solution.py
@@ -129,6 +129,12 @@
 
     receive(y)
     forward(y).start()
+    for i in range(2):
+        @pl.when((across(i) == 1) & jnp.logical_not(same))
+        def _(i=i):
+            send(1 - i).wait_send()
+            send(i).start()
+
     for copy in small_copies:
         copy.wait()
     diagonal = lax.broadcasted_iota(jnp.int32, (HD, HD), 0) == lax.broadcasted_iota(jnp.int32, (HD, HD), 1)
@@ -190,12 +196,6 @@
     work(0)
     pl.semaphore_wait(stages.at[1], 1)
     tell(stages.at[2], beside)
-
-    for i in range(2):
-        @pl.when((across(i) == 1) & jnp.logical_not(same))
-        def _(i=i):
-            send(1 - i).wait_send()
-            send(i).start()
 
 
     my_rows = pl.ds(pl.multiple_of(f_me * 16, 16), 16)

time: 107 us -> 106 us (level)
  no operation moved by 1% of the time
where the time goes in v3:
time: 106 us
  Pallas kernels  102 us (96%)
  other arithmetic  1.37 us (1%)
  local copies, waits for them, and re-layouts  1.1 us (1%)
    pallas_call x1, Pallas kernels, block_call(): pl.pallas_call(functools.partial(block_kernel, exact=exact), out_shape=ja...  102 us

profile of v3, /device:TPU:0, one launch (start us, length us, event | category | flops | bytes accessed | tf_op | source)
XLA Modules:
  0.0 106.2 jit_solution(11307863401373122267)
XLA Ops:
  0.0 1.4 %abs_reduce_fusion = f32[]{:T(128)} fusion(f32[2,2,72]{2,1,0:T(2,128)} %param.15), kind=kLoop, calls=%fused_computation | loop fusion | flops 431 | bytes 1156 | tf_op jit(solution)/shard_map/reduce_max | solution.py:416
  2.0 103.0 %conditional.1 = (bf16[16,2,2,8,1152]{4,3,2,1,0:T(8,128)(2,1)S(1)}) conditional(s32[]{:T(128)} %convert_element_type.3, (bf16[2,256,1152]{2,1,0:T(8,128)(2,1)}, f32[3,2,1152]{2,1,0:T(2,128)}, f32[2,2,72]{2,1,0:T(2,128)}, bf16[1152,3456]{1,0:T(8,128)(2,1)}, bf16[1152,1152]{1,0:T(8,128)(2,1)}, /*index=5*/bf16[1152,3456]{1,0:T(8,128)(2,1)}, ...), branch_computations={%region_1.0_spmd, %region_2.0_spmd} | conditional | bytes 8 | solution.py:417
  2.0 102.5 %block_exact.1 = bf16[16,2,2,8,1152]{4,3,2,1,0:T(8,128)(2,1)S(1)} custom-call(bf16[2,256,1152]{2,1,0:T(8,128)(2,1)} %get-tuple-element.36.frames, f32[3,2,1152]{2,1,0:T(2,128)} %get-tuple-element.37.modulation_in, f32[2,2,72]{2,1,0:T(2,128)} %get-tuple-element.38.gains_in, bf16[1152,3456]{1,0:T(8,128)(2,1)} %get-tuple-element.39.w_qkv, ...), custom_call_target="tpu_custom_call" | custom-call | tf_op jit(solution)/shard_map/cond/branch_0_fun/block_exact/pallas_call | solution.py:381
  105.0 1.1 %copy.8 = bf16[2,16,2,8,1152]{4,3,2,1,0:T(8,128)(2,1)} copy(bf16[2,16,2,8,1152]{4,3,0,2,1:T(8,128)(2,1)S(1)} %bitcast.3) | data formatting | bytes 2359296 | tf_op jit(solution)/shard_map/transpose | solution.py:420
